TPU v7x, 32 devices: a whole 2x2x4 slice. The times are simulated.
32 devices in a mesh: row: 16 (over z, y, x), col: 2 (over core).
Axes of the slice: x: 2, y: 2, z: 4, core: 2. Of those that a mesh axis runs over, the one named last changes fastest.
Arguments:
- vectors: float32 [6144, 64], P(('row', 'col')), may hold values from -6 to 6
- stiff_tiles: float32 [16, 2, 32, 192, 192], P('row', 'col'), may hold values from -0.078125 to 0.078125
- tile_coords: int32 [16, 2, 32, 2], P('row', 'col'), may hold values from 0 to 15, as said below
- tile_valid: int32 [16, 2, 32], P('row', 'col'), may hold values from 0 to 1, as said below
Outputs:
- product: float32 [6144, 64], P(('row', 'col'))
Inputs may be any that keep to these rules, and one draw needn't show every extreme that they name: `tile_coords`: valid entries of a device's list are distinct and come before all padding; each list holds at most 32 valid entries, and some list holds exactly 32. A stored tile may lie on either side of the diagonal. Padding entries hold in-range coordinates. `tile_valid`: at least one entry of each list is valid.
All inputs are finite; a program needn't handle non-finite values.
Results may differ from a plain program's by a relative error of at most 0.0001.
Values sent between devices are 32-bit elements; how exact they have to be, the bound alone decides.
A program may use at most 128 MiB of HBM per device.

v0:
```python
import jax
import jax.numpy as jnp
from jax import lax
from jax.sharding import PartitionSpec as P

ITERS = 2
GROUP = 8


def local(vectors, stiff_tiles, tile_coords, tile_valid):
    row_count = lax.axis_size("row")
    column_count = lax.axis_size("col")
    tile_size = stiff_tiles.shape[-1]
    vector_count = vectors.shape[1]
    blocks_here = vectors.shape[0] // tile_size
    span_rows = blocks_here * column_count
    span_cols = blocks_here * row_count
    row_pos = lax.axis_index("row")
    col_pos = lax.axis_index("col")
    local_tiles = stiff_tiles[0, 0]
    local_rows = tile_coords[0, 0, :, 0]
    local_cols = tile_coords[0, 0, :, 1]
    live_mask = tile_valid[0, 0].astype(jnp.float32)
    global_row = row_pos * span_rows + local_rows
    global_col = (
        local_cols // blocks_here * column_count + col_pos
    ) * blocks_here + local_cols % blocks_here
    mirror = live_mask * (global_row != global_col).astype(jnp.float32)
    rows_hot = (local_rows[:, None] == jnp.arange(span_rows, dtype=jnp.int32)[None, :]).astype(
        jnp.float32
    ) * live_mask[:, None]
    cols_hot = (local_cols[:, None] == jnp.arange(span_cols, dtype=jnp.int32)[None, :]).astype(
        jnp.float32
    ) * mirror[:, None]
    slot_count = local_tiles.shape[0]
    turn_count = slot_count // GROUP
    current = vectors
    for repeat in range(ITERS):
        everything = lax.all_gather(current, ("row", "col"), axis=0, tiled=True)
        blocks = everything.reshape(row_count, column_count, blocks_here, tile_size, vector_count)
        col_panel = lax.dynamic_index_in_dim(blocks, col_pos, 1, keepdims=False).reshape(
            span_cols, tile_size, vector_count
        )
        row_panel = lax.dynamic_index_in_dim(blocks, row_pos, 0, keepdims=False).reshape(
            span_rows, tile_size, vector_count
        )

        def one_turn(turn, partials):
            row_part, col_part = partials
            first_slot = turn * GROUP
            tile_batch = lax.dynamic_slice_in_dim(local_tiles, first_slot, GROUP, 0)
            batch_rows = lax.dynamic_slice_in_dim(local_rows, first_slot, GROUP, 0)
            batch_cols = lax.dynamic_slice_in_dim(local_cols, first_slot, GROUP, 0)
            pick_rows = lax.dynamic_slice_in_dim(rows_hot, first_slot, GROUP, 0)
            pick_cols = lax.dynamic_slice_in_dim(cols_hot, first_slot, GROUP, 0)
            right_side = jnp.take(col_panel, batch_cols, axis=0)
            left_side = jnp.take(row_panel, batch_rows, axis=0)
            direct = jnp.einsum(
                "gpq,gqk->gpk", tile_batch, right_side, precision=lax.Precision.HIGHEST
            )
            mirrored = jnp.einsum(
                "gqp,gqk->gpk", tile_batch, left_side, precision=lax.Precision.HIGHEST
            )
            row_part = row_part + jnp.einsum(
                "ga,gpk->apk", pick_rows, direct, precision=lax.Precision.HIGHEST
            )
            col_part = col_part + jnp.einsum(
                "gb,gpk->bpk", pick_cols, mirrored, precision=lax.Precision.HIGHEST
            )
            return (row_part, col_part)

        start_value = (
            jnp.zeros((span_rows, tile_size, vector_count), jnp.float32),
            jnp.zeros((span_cols, tile_size, vector_count), jnp.float32),
        )
        row_part, col_part = lax.fori_loop(0, turn_count, one_turn, start_value)
        own_rows = lax.psum_scatter(
            row_part.reshape(span_rows * tile_size, vector_count),
            "col",
            scatter_dimension=0,
            tiled=True,
        )
        own_cols = lax.psum_scatter(
            col_part.reshape(span_cols * tile_size, vector_count),
            "row",
            scatter_dimension=0,
            tiled=True,
        )
        current = own_rows + own_cols
    return current


def solution(mesh):
    placed = (
        P(("row", "col"), None),
        P("row", "col", None, None, None),
        P("row", "col", None, None),
        P("row", "col", None),
    )
    return jax.shard_map(
        local, mesh=mesh, in_specs=placed, out_specs=P(("row", "col"), None), check_vma=False
    )
```

profile of v0, /device:TPU:0, one launch (start us, length us, event | category | flops | bytes accessed | tf_op | source)
XLA Modules:
  0.0 509.4 jit_solution(7517432324821061954)
XLA Ops:
  9.6 59.7 %all-gather.5.cloned.1.call-done = f32[32,192,64]{1,2,0:T(8,128)} async-done(((f32[1,192,64]{1,2,0:T(8,128)}), f32[32,192,64]{1,2,0:T(8,128)}) %all-gather.5.cloned.1.call-update) | async-done | bytes 1572880 | tf_op jit(solution)/shard_map/all_gather | solution.py:39
  73.3 44.9 %while.32 = (s32[]{:T(128)}, f32[2,192,64]{1,0,2:T(2,128)S(1)}, f32[16,192,64]{1,0,2:T(8,128)S(1)}, f32[32,2]{0,1:T(2,128)S(1)}, f32[32,192,192]{2,1,0:T(8,128)}...) while((s32[]{:T(128)}, f32[2,192,64]{1,0,2:T(2,128)S(1)}, ...), condition=%wide.region_1.4_spmd.clone, body=%wide.region_0.3_spmd.clone.sunk | while | flops 474859616 | bytes 9253618 | solution.py:76
  74.1 3.0 fusion.74
  80.6 3.0 fusion.73
  85.3 3.0 fusion.74
  91.8 3.0 fusion.73
  96.5 3.0 fusion.74
  103.0 3.0 fusion.73
  107.7 3.0 fusion.74
  114.2 3.0 fusion.73
  121.0 4.6 reduce-scatter.13.cloned.1.call-done
  126.6 129.6 %reduce-scatter.15.cloned.1.call-done = f32[192,64]{1,0:T(8,128)} async-done(((f32[3072,64]{1,0:T(8,128)}), f32[192,64]{1,0:T(8,128)}) %reduce-scatter.15.cloned.1.call-update) | async-done | bytes 49168
  258.1 56.1 %all-gather.7.cloned.1.call-done = f32[32,192,64]{1,2,0:T(8,128)} async-done(((f32[1,192,64]{1,2,0:T(8,128)}), f32[32,192,64]{1,2,0:T(8,128)}) %all-gather.7.cloned.1.call-update) | async-done | bytes 1572880 | tf_op jit(solution)/shard_map/all_gather | solution.py:39
  318.3 44.9 %while.33 = (s32[]{:T(128)}, f32[2,192,64]{1,0,2:T(2,128)S(1)}, f32[16,192,64]{1,0,2:T(8,128)S(1)}, f32[32,2]{0,1:T(2,128)S(1)}, f32[32,192,192]{2,1,0:T(8,128)}...) while((s32[]{:T(128)}, f32[2,192,64]{1,0,2:T(2,128)S(1)}, ...), condition=%wide.region_5.8_spmd.clone, body=%wide.region_4.7_spmd.clone.sunk | while | flops 474859616 | bytes 9253618 | solution.py:76
  319.0 3.0 fusion.84
  325.5 3.0 fusion.83
  330.2 3.0 fusion.84
  336.7 3.0 fusion.83
  341.4 3.0 fusion.84
  347.9 3.0 fusion.83
  352.6 3.0 fusion.84
  359.1 3.0 fusion.83
  365.9 4.7 reduce-scatter.17.cloned.1.call-done
  371.5 129.4 %reduce-scatter.19.cloned.1.call-done = f32[192,64]{1,0:T(8,128)} async-done(((f32[3072,64]{1,0:T(8,128)}), f32[192,64]{1,0:T(8,128)}) %reduce-scatter.19.cloned.1.call-update) | async-done | bytes 49168
  (95 shorter events, 63.0 us)
Async XLA Ops:
  6.5 62.8 %all-gather.5.cloned.1.call-start = ((), (), s32[]{:S(2)}) async-start(), calls=%async_computation.4 | async-start | bytes 2162688 | tf_op jit(solution)/shard_map/all_gather | solution.py:39
  7.3 118.4 %reduce-scatter.13.cloned.1.call-start = ((), (), s32[]{:S(2)}) async-start(), calls=%async_computation.6 | async-start | bytes 294912
  119.1 137.2 %reduce-scatter.15.cloned.1.call-start = ((), (), s32[]{:S(2)}) async-start(), calls=%async_computation.7 | async-start | bytes 1671168
  121.0 193.3 %all-gather.7.cloned.1.call-start = ((), (), s32[]{:S(2)}) async-start(), calls=%async_computation.5 | async-start | bytes 2162688 | tf_op jit(solution)/shard_map/all_gather | solution.py:39
  257.8 112.7 %reduce-scatter.17.cloned.1.call-start = ((), (), s32[]{:S(2)}) async-start(), calls=%async_computation.8 | async-start | bytes 294912
  364.0 137.0 %reduce-scatter.19.cloned.1.call-start = ((), (), s32[]{:S(2)}) async-start(), calls=%async_computation.9 | async-start | bytes 1671168
Sparse Core Ops, SparseCore 0:
  10.2 59.0 all-gather.4
  119.2 6.4 reduce-scatter.12
  130.4 125.7 reduce-scatter.14
  258.9 55.2 all-gather.6
  364.1 6.4 reduce-scatter.16
  375.2 125.7 reduce-scatter.18
where the time goes:
time: 510 us; the launch traced here: 509 us
  waiting for transfers between devices  385 us (75%)
  matrix products  67.6 us (13%)
  local copies, waits for them, and re-layouts  38.7 us (8%)
  between operations  13.6 us (3%)
    unnamed x10, waiting for transfers between devices  269 us
    all_gather x2, waiting for transfers between devices, local(): everything = lax.all_gather(current, ('row', 'col'), axis=0, tiled=True)  116 us
    dot_general x8, matrix products, one_turn(): jnp.einsum('gpq,gqk->gpk', tile_batch, right_side, precision=lax.Precisio...  24 us
    dot_general x8, matrix products, one_turn(): jnp.einsum('gqp,gqk->gpk', tile_batch, left_side, precision=lax.Precision...  24 us
    gather x8, local copies, waits for them, and re-layouts, one_turn(): right_side = jnp.take(col_panel, batch_cols, axis=0)  16 us
    dot_general x8, matrix products, one_turn(): jnp.einsum('gb,gpk->bpk', pick_cols, mirrored, precision=lax.Precision.HI...  11.5 us
  transfers between devices with their start and end apart: 6, of which 6 were waited for; matrix products, arithmetic and copies ran while one was open for 2% of the time, Pallas kernels for 0%

commit v1 on v0

v1 whole, which is shorter than its diff:
```python
import functools

import jax
import jax.numpy as jnp
from jax import lax
from jax.experimental import pallas as pl
from jax.experimental.pallas import tpu as pltpu
from jax.sharding import PartitionSpec as P

ITERS = 2
MESH = pl.DeviceIdType.MESH
LANES = 128


def split(value):
    high = value.astype(jnp.bfloat16).astype(jnp.float32)
    return high, value - high


def pack_tall(value):
    half = value.shape[0] // 2
    return jnp.concatenate([value[:half], value[half:]], axis=1)


def spread(packed):
    high, low = split(packed)
    width = packed.shape[1] // 2
    left = lax.broadcasted_iota(jnp.int32, packed.shape, 1) < width
    upper = jnp.where(left, high, pltpu.roll(low, width, 1))
    lower = jnp.where(left, pltpu.roll(high, width, 1), low)
    return jnp.concatenate([upper, lower], axis=0)


def fold_tall(total):
    width = total.shape[1] // 2
    half = total.shape[0] // 2
    folded = total + pltpu.roll(total, width, 1)
    left = lax.broadcasted_iota(jnp.int32, (half, total.shape[1]), 1) < width
    return jnp.where(left, folded[:half], folded[half:])


def unpack_wide(packed, vecs, size):
    main = packed[:vecs].T
    tail = packed[vecs:]
    tail = jnp.concatenate([tail[:, : size - LANES], tail[:, size - LANES :]], axis=0).T
    return jnp.concatenate([main, tail], axis=0)


def kernel(
    rows, cols, planes,
    x_ref, slot_ref, tiles_hbm, out_ref,
    tiles, gath, rowg, rpart, rrecv, zsend, zrecv, z2send, z2recv, lhs, total,
    tile_sem, ag_send, ag_recv, cx_send, cx_recv, r1_send, r1_recv, r2_send, r2_recv,
    cy_send, cy_recv,
):
    lines = rows // planes
    size, vecs = x_ref.shape
    row = lax.axis_index("row")
    col = lax.axis_index("col")
    line = row // planes
    plane = row % planes

    load = pltpu.make_async_copy(tiles_hbm, tiles, tile_sem)
    load.start()

    def line_peer(dz):
        return (((line + dz) % lines) * planes + plane, col)

    def plane_peer(d):
        return (line * planes + (plane + d) % planes, col)

    def col_peer(dc):
        return (row, (col + dc) % cols)

    def remote(src, dst, send, recv, where):
        return pltpu.make_async_remote_copy(
            src_ref=src, dst_ref=dst, send_sem=send, recv_sem=recv,
            device_id=where, device_id_type=MESH,
        )

    def ag_line(it, dz):
        return remote(gath.at[it, 0, 0], gath.at[it, dz, 0],
                      ag_send.at[it, dz, 0], ag_recv.at[it, dz, 0], line_peer(dz))

    def ag_plane(it, dz, d):
        return remote(gath.at[it, dz, 0], gath.at[it, dz, d],
                      ag_send.at[it, dz, d], ag_recv.at[it, dz, d], plane_peer(d))

    def col_x(it, dc):
        return remote(gath.at[it, 0, 0], rowg.at[it, dc],
                      cx_send.at[it, dc], cx_recv.at[it, dc], col_peer(dc))

    def rs_plane(it, dz, d):
        return remote(zsend.at[it, dz, d], zrecv.at[it, dz, d],
                      r1_send.at[it, dz, d], r1_recv.at[it, dz, d], plane_peer(d))

    def rs_line(it, dz):
        return remote(z2send.at[it, dz], z2recv.at[it, dz],
                      r2_send.at[it, dz], r2_recv.at[it, dz], line_peer(dz))

    def col_y(it, dc):
        return remote(rpart.at[it, dc], rrecv.at[it, dc],
                      cy_send.at[it, dc], cy_recv.at[it, dc], col_peer(dc))

    barrier = pltpu.get_barrier_semaphore()
    for dz in range(1, lines):
        pl.semaphore_signal(barrier, inc=1, device_id=line_peer(dz), device_id_type=MESH)
    for d in range(1, planes):
        pl.semaphore_signal(barrier, inc=1, device_id=plane_peer(d), device_id_type=MESH)
    for dc in range(1, cols):
        pl.semaphore_signal(barrier, inc=1, device_id=col_peer(dc), device_id_type=MESH)
    first = pack_tall(x_ref[...])
    gath[0, 0, 0] = first
    pl.semaphore_wait(barrier, (lines - 1) + (planes - 1) + (cols - 1))

    def tile_parts(a, b, keep):
        slot = slot_ref[a * rows + b]
        scale = jnp.where(slot >= 0, 1.0, 0.0).astype(jnp.float32) * keep
        block = tiles[jnp.maximum(slot, 0)] * scale
        high = block.astype(jnp.bfloat16)
        low = (block - high.astype(jnp.float32)).astype(jnp.bfloat16)
        return high, low

    def mirrored(it, dz, d):
        b = ((line + dz) % lines) * planes + (plane + d) % planes
        acc = jnp.zeros((2 * vecs, size), jnp.float32)
        for dc in range(cols):
            a = (col - dc + cols) % cols
            keep = jnp.where(b == row, 0.0, 1.0).astype(jnp.float32) if dc == 0 else 1.0
            high, low = tile_parts(a, b, keep)
            left = lhs[dc]
            acc = acc + jnp.dot(left, high, preferred_element_type=jnp.float32)
            acc = acc + jnp.dot(left, low, preferred_element_type=jnp.float32)
        wide = acc[:vecs] + acc[vecs:]
        tail = wide[:, LANES:]
        zsend[it, dz, d, pl.ds(0, vecs), :] = wide[:, :LANES]
        zsend[it, dz, d, pl.ds(vecs, vecs // 2), :] = jnp.concatenate(
            [tail[: vecs // 2], tail[vecs // 2 :]], axis=1
        )

    def direct(it, dz, d):
        b = ((line - dz + lines) % lines) * planes + (plane - d + planes) % planes
        right = spread(gath[it, dz, d]).astype(jnp.bfloat16)
        for dc in range(cols):
            a = (col + dc) % cols
            high, low = tile_parts(a, b, 1.0)
            total[dc] += jnp.dot(high, right, preferred_element_type=jnp.float32) + jnp.dot(
                low, right, preferred_element_type=jnp.float32
            )

    def product(it):
        for dc in range(1, cols):
            col_x(it, dc).start()
        for dz in range(1, lines):
            ag_line(it, dz).start()
        for d in range(1, planes):
            ag_plane(it, 0, d).start()
        lhs[0] = spread(gath[it, 0, 0]).T.astype(jnp.bfloat16)
        for dc in range(1, cols):
            col_x(it, dc).wait_recv()
            lhs[dc] = spread(rowg[it, dc]).T.astype(jnp.bfloat16)
        total[...] = jnp.zeros_like(total)

        def group(dz, carry):
            @pl.when(dz > 0)
            def _():
                ag_line(it, dz).wait_recv()
                for d in range(1, planes):
                    ag_plane(it, dz, d).start()

            def one(d, inner):
                mirrored(it, dz, d)
                rs_plane(it, dz, d).start()
                return inner

            return lax.fori_loop(1, planes, one, carry)

        if True:
            group_first = group
            lax.fori_loop(0, lines, group_first, 0)

        def own(dz, carry):
            mirrored(it, dz, 0)
            direct(it, dz, 0)
            return carry

        lax.fori_loop(0, lines, own, 0)

        def reduce(k, carry):
            dz = lines - 1 - k
            block = zsend[it, dz, 0]
            for d in range(1, planes):
                rs_plane(it, dz, d).wait_recv()
                block = block + zrecv[it, dz, d]
            z2send[it, dz] = block

            @pl.when(dz > 0)
            def _():
                rs_line(it, dz).start()

            return carry

        lax.fori_loop(0, lines, reduce, 0)

        def rest(dz, carry):
            def one(d, inner):
                ag_plane(it, dz, d).wait_recv()
                direct(it, dz, d)
                return inner

            return lax.fori_loop(1, planes, one, carry)

        lax.fori_loop(0, lines, rest, 0)

        for dc in range(1, cols):
            rpart[it, dc] = fold_tall(total[dc])
            col_y(it, dc).start()
        mine = fold_tall(total[0])
        wide = z2send[it, 0]
        for dz in range(1, lines):
            rs_line(it, dz).wait_recv()
            wide = wide + z2recv[it, dz]
        tall = unpack_wide(wide, vecs, size)
        for dc in range(1, cols):
            col_y(it, dc).wait_recv()
            mine = mine + rrecv[it, dc]
        return mine, tall

    def step(it, carry):
        mine, tall = product(it)

        @pl.when(it < ITERS - 1)
        def _():
            gath[lax.rem(it + 1, ITERS), 0, 0] = mine + pack_tall(tall)

        @pl.when(it == ITERS - 1)
        def _():
            half = size // 2
            out_ref[pl.ds(0, half), :] = mine[:, :vecs] + tall[:half]
            out_ref[pl.ds(half, half), :] = mine[:, vecs:] + tall[half:]

        return carry

    load.wait()
    lax.fori_loop(0, ITERS, step, 0)

    def drain(it, carry):
        for dc in range(1, cols):
            col_x(it, dc).wait_send()
            col_y(it, dc).wait_send()
        for dz in range(1, lines):
            ag_line(it, dz).wait_send()
            rs_line(it, dz).wait_send()

        def plane_sends(dz, inner):
            for d in range(1, planes):
                ag_plane(it, dz, d).wait_send()
                rs_plane(it, dz, d).wait_send()
            return inner

        return lax.fori_loop(0, lines, plane_sends, carry)

    lax.fori_loop(0, ITERS, drain, 0)


def local(rows, cols, vectors, stiff_tiles, tile_coords, tile_valid):
    size, vecs = vectors.shape
    count = stiff_tiles.shape[2]
    planes = 4 if rows % 4 == 0 else 1
    lines = rows // planes
    place = tile_coords[0, 0, :, 0] * rows + tile_coords[0, 0, :, 1]
    hit = (place[None, :] == jnp.arange(rows * cols, dtype=jnp.int32)[:, None]) & (
        tile_valid[0, 0][None, :] > 0
    )
    slots = jnp.max(jnp.where(hit, jnp.arange(count, dtype=jnp.int32)[None, :], -1), axis=1)
    block = (size * vecs // LANES, LANES)
    f32 = jnp.float32
    dma = pltpu.SemaphoreType.DMA
    grid = (ITERS, lines, planes)
    return pl.pallas_call(
        functools.partial(kernel, rows, cols, planes),
        out_shape=jax.ShapeDtypeStruct((size, vecs), f32),
        in_specs=[
            pl.BlockSpec(memory_space=pltpu.VMEM),
            pl.BlockSpec(memory_space=pltpu.SMEM),
            pl.BlockSpec(memory_space=pl.ANY),
        ],
        out_specs=pl.BlockSpec(memory_space=pltpu.VMEM),
        scratch_shapes=[
            pltpu.VMEM((count, size, size), f32),
            pltpu.VMEM(grid + block, f32),
            pltpu.VMEM((ITERS, cols) + block, f32),
            pltpu.VMEM((ITERS, cols) + block, f32),
            pltpu.VMEM((ITERS, cols) + block, f32),
            pltpu.VMEM(grid + block, f32),
            pltpu.VMEM(grid + block, f32),
            pltpu.VMEM((ITERS, lines) + block, f32),
            pltpu.VMEM((ITERS, lines) + block, f32),
            pltpu.VMEM((cols, 2 * vecs, size), jnp.bfloat16),
            pltpu.VMEM((cols, size, 2 * vecs), f32),
            dma,
            dma(grid), dma(grid),
            dma((ITERS, cols)), dma((ITERS, cols)),
            dma(grid), dma(grid),
            dma((ITERS, lines)), dma((ITERS, lines)),
            dma((ITERS, cols)), dma((ITERS, cols)),
        ],
        compiler_params=pltpu.CompilerParams(
            collective_id=0, has_side_effects=True, vmem_limit_bytes=48 * 1024 * 1024
        ),
    )(vectors, slots, stiff_tiles[0, 0])


def solution(mesh):
    placed = (
        P(("row", "col"), None),
        P("row", "col", None, None, None),
        P("row", "col", None, None),
        P("row", "col", None),
    )
    return jax.shard_map(
        functools.partial(local, mesh.shape["row"], mesh.shape["col"]),
        mesh=mesh, in_specs=placed, out_specs=P(("row", "col"), None), check_vma=False,
    )
```

time: 510 us -> 61.6 us (0.12)
  waiting for transfers between devices: 385 us -> 0 us
  matrix products: 67.6 us -> 0 us
  Pallas kernels: 0 us -> 58.2 us
  local copies, waits for them, and re-layouts: 38.7 us -> 1.65 us
  between operations: 13.6 us -> 0.01 us
    unnamed x10 -> x0, waiting for transfers between devices: 269 us -> none
    all_gather x2 -> x0, waiting for transfers between devices: 116 us -> none  [local(): everything = lax.all_gather(current, ('row', 'col'), axis=0, tiled=True)]
    dot_general x32 -> x0, matrix products: 67.6 us -> none  [the longest x8 24 us: one_turn(): jnp.einsum('gpq,gqk->gpk', tile_batch, right_side, precision=lax.Precisio...]
    pallas_call x0 -> x1, Pallas kernels: none -> 58.2 us  [local(): pl.pallas_call(functools.partial(kernel, rows, cols, planes), out_shape=j...]
    gather x16 -> x0, local copies, waits for them, and re-layouts: 20.8 us -> none  [the longest x8 16 us: one_turn(): right_side = jnp.take(col_panel, batch_cols, axis=0)]
    unnamed x8 -> x1, local copies, waits for them, and re-layouts: 9.11 us -> 0.94 us
    dynamic_slice x8 -> x0, local copies, waits for them, and re-layouts: 8.01 us -> none  [the longest x4 5.96 us: local(): lax.dynamic_index_in_dim(blocks, col_pos, 1, keepdims=False)]
  transfers between devices with their start and end apart: 6 -> 0, of which waited for: 6 -> 0; matrix products, arithmetic and copies ran while one was open for 2% -> 0% of each run, Pallas kernels for 0% -> 0%
where the time goes in v1:
time: 61.6 us; the launch traced here: 61.4 us
  Pallas kernels  58.2 us (94%)
  local copies, waits for them, and re-layouts  1.65 us (3%)
  other arithmetic  1.53 us (2%)
    pallas_call x1, Pallas kernels, local(): pl.pallas_call(functools.partial(kernel, rows, cols, planes), out_shape=j...  58.2 us

profile of v1, /device:TPU:0, one launch (start us, length us, event | category | flops | bytes accessed | tf_op | source)
XLA Modules:
  0.0 61.4 jit_solution(4252537189038643020)
XLA Ops:
  0.0 0.8 %add_bitcast_fusion = s32[32]{0:T(128)S(1)} fusion(s32[1,1,32,2]{2,3,1,0:T(2,128)} %param.6), kind=kLoop, calls=%fused_computation.4 | loop fusion | flops 64 | bytes 384 | tf_op jit(solution)/shard_map/add | solution.py:271
  0.8 0.7 %compare_bitcast_fusion = pred[32]{0:T(512)(128)(4,1)S(1)} fusion(s32[1,1,32]{2,1,0:T(1,128)} %param.7), kind=kLoop, calls=%fused_computation.3 | loop fusion | flops 32 | bytes 160 | tf_op jit(solution)/shard_map/gt | solution.py:273
  1.4 0.1 select_reduce_fusion.slot_ref
  1.5 0.9 %copy.7.x_ref = f32[192,64]{1,0:T(8,128)S(1)} copy(f32[192,64]{0,1:T(8,128)} %param.4) | data formatting | bytes 98304 | tf_op args[0]
  2.5 58.2 %shard_map.46 = f32[192,64]{1,0:T(8,128)S(1)} custom-call(f32[192,64]{1,0:T(8,128)S(1)} %copy.7.x_ref, s32[32]{0:T(128)S(1)} %select_reduce_fusion.slot_ref, f32[32,192,192]{2,1,0:T(8,128)} %bitcast.5), custom_call_target="tpu_custom_call" | custom-call | tf_op jit(solution)/shard_map/pallas_call | solution.py:280
  60.7 0.7 %copy.8 = f32[192,64]{0,1:T(8,128)} copy(f32[192,64]{1,0:T(8,128)S(1)} %shard_map.46) | data formatting | bytes 98304 | tf_op jit(solution)/shard_map/pallas_call | solution.py:280

commit v2 on v1

--- a/solution.py
+++ b/solution.py
@@ -50,24 +50,37 @@
     rows, cols, planes,
     x_ref, slot_ref, tiles_hbm, out_ref,
     tiles, gath, rowg, rpart, rrecv, zsend, zrecv, z2send, z2recv, lhs, total,
-    tile_sem, ag_send, ag_recv, cx_send, cx_recv, r1_send, r1_recv, r2_send, r2_recv,
+    tile_sem, ag_send, ag_recv, at_send, at_recv, cx_send, cx_recv, r1_send, r1_recv, rt_send, rt_recv, r2_send, r2_recv,
     cy_send, cy_recv,
 ):
     lines = rows // planes
-    size, vecs = x_ref.shape
+    vecs, size = x_ref.shape
+    half = size // 2
+    quarter = half // 2
     row = lax.axis_index("row")
     col = lax.axis_index("col")
     line = row // planes
     plane = row % planes
+    up = plane // 2
+    side = plane % 2
 
     load = pltpu.make_async_copy(tiles_hbm, tiles, tile_sem)
     load.start()
 
+    def flipped(d):
+        if d == 0:
+            return plane
+        if d == 1:
+            return up * 2 + 1 - side
+        if d == 2:
+            return (1 - up) * 2 + side
+        return (1 - up) * 2 + 1 - side
+
     def line_peer(dz):
         return (((line + dz) % lines) * planes + plane, col)
 
     def plane_peer(d):
-        return (line * planes + (plane + d) % planes, col)
+        return (line * planes + flipped(d), col)
 
     def col_peer(dc):
         return (row, (col + dc) % cols)
@@ -86,10 +99,20 @@
         return remote(gath.at[it, dz, 0], gath.at[it, dz, d],
                       ag_send.at[it, dz, d], ag_recv.at[it, dz, d], plane_peer(d))
 
+    def ag_turn(it, dz, h):
+        part = pl.ds(h * quarter, quarter)
+        return remote(gath.at[it, dz, 1 + h, part], gath.at[it, dz, 3, part],
+                      at_send.at[it, dz, h], at_recv.at[it, dz, h], plane_peer(2 - h))
+
     def col_x(it, dc):
         return remote(gath.at[it, 0, 0], rowg.at[it, dc],
                       cx_send.at[it, dc], cx_recv.at[it, dc], col_peer(dc))
 
+    def rs_turn(it, dz, h):
+        part = pl.ds(h * quarter, quarter)
+        return remote(zsend.at[it, dz, 3, part], zrecv.at[it, dz, 3, part],
+                      rt_send.at[it, dz, h], rt_recv.at[it, dz, h], plane_peer(1 + h))
+
     def rs_plane(it, dz, d):
         return remote(zsend.at[it, dz, d], zrecv.at[it, dz, d],
                       r1_send.at[it, dz, d], r1_recv.at[it, dz, d], plane_peer(d))
@@ -105,13 +128,14 @@
     barrier = pltpu.get_barrier_semaphore()
     for dz in range(1, lines):
         pl.semaphore_signal(barrier, inc=1, device_id=line_peer(dz), device_id_type=MESH)
-    for d in range(1, planes):
+    for d in range(1, 3):
         pl.semaphore_signal(barrier, inc=1, device_id=plane_peer(d), device_id_type=MESH)
     for dc in range(1, cols):
         pl.semaphore_signal(barrier, inc=1, device_id=col_peer(dc), device_id_type=MESH)
-    first = pack_tall(x_ref[...])
-    gath[0, 0, 0] = first
-    pl.semaphore_wait(barrier, (lines - 1) + (planes - 1) + (cols - 1))
+    gath[0, 0, 0] = pack_tall(
+        jnp.concatenate([x_ref[:, :LANES].T, x_ref[:, LANES:].T], axis=0)
+    )
+    pl.semaphore_wait(barrier, (lines - 1) + 2 + (cols - 1))
 
     def tile_parts(a, b, keep):
         slot = slot_ref[a * rows + b]
@@ -122,7 +146,7 @@
         return high, low
 
     def mirrored(it, dz, d):
-        b = ((line + dz) % lines) * planes + (plane + d) % planes
+        b = ((line + dz) % lines) * planes + flipped(d)
         acc = jnp.zeros((2 * vecs, size), jnp.float32)
         for dc in range(cols):
             a = (col - dc + cols) % cols
@@ -133,13 +157,16 @@
             acc = acc + jnp.dot(left, low, preferred_element_type=jnp.float32)
         wide = acc[:vecs] + acc[vecs:]
         tail = wide[:, LANES:]
-        zsend[it, dz, d, pl.ds(0, vecs), :] = wide[:, :LANES]
-        zsend[it, dz, d, pl.ds(vecs, vecs // 2), :] = jnp.concatenate(
-            [tail[: vecs // 2], tail[vecs // 2 :]], axis=1
+        return jnp.concatenate(
+            [
+                wide[:, :LANES],
+                jnp.concatenate([tail[: vecs // 2], tail[vecs // 2 :]], axis=1),
+            ],
+            axis=0,
         )
 
     def direct(it, dz, d):
-        b = ((line - dz + lines) % lines) * planes + (plane - d + planes) % planes
+        b = ((line - dz + lines) % lines) * planes + flipped(d)
         right = spread(gath[it, dz, d]).astype(jnp.bfloat16)
         for dc in range(cols):
             a = (col + dc) % cols
@@ -149,38 +176,60 @@
             )
 
     def product(it):
-        for dc in range(1, cols):
-            col_x(it, dc).start()
         for dz in range(1, lines):
             ag_line(it, dz).start()
-        for d in range(1, planes):
+        for dc in range(1, cols):
+            col_x(it, dc).start()
+        for d in range(1, 3):
             ag_plane(it, 0, d).start()
         lhs[0] = spread(gath[it, 0, 0]).T.astype(jnp.bfloat16)
         for dc in range(1, cols):
             col_x(it, dc).wait_recv()
             lhs[dc] = spread(rowg[it, dc]).T.astype(jnp.bfloat16)
         total[...] = jnp.zeros_like(total)
+
+        @pl.when(it == 0)
+        def _():
+            load.wait()
+
+        def corner(dz, carry):
+            zsend[it, dz, 3] = mirrored(it, dz, 3)
+            for h in range(2):
+                rs_turn(it, dz, h).start()
+            return carry
+
+        lax.fori_loop(0, lines, corner, 0)
 
         def group(dz, carry):
             @pl.when(dz > 0)
             def _():
                 ag_line(it, dz).wait_recv()
-                for d in range(1, planes):
+                for d in range(1, 3):
                     ag_plane(it, dz, d).start()
 
-            def one(d, inner):
-                mirrored(it, dz, d)
-                rs_plane(it, dz, d).start()
-                return inner
-
-            return lax.fori_loop(1, planes, one, carry)
-
-        if True:
-            group_first = group
-            lax.fori_loop(0, lines, group_first, 0)
+            one = mirrored(it, dz, 1)
+            rs_turn(it, dz, 1).wait_recv()
+            zsend[it, dz, 1, pl.ds(0, quarter), :] = one[:quarter]
+            zsend[it, dz, 1, pl.ds(quarter, quarter), :] = (
+                one[quarter:] + zrecv[it, dz, 3, pl.ds(quarter, quarter), :]
+            )
+            rs_plane(it, dz, 1).start()
+            two = mirrored(it, dz, 2)
+            rs_turn(it, dz, 0).wait_recv()
+            zsend[it, dz, 2, pl.ds(0, quarter), :] = (
+                two[:quarter] + zrecv[it, dz, 3, pl.ds(0, quarter), :]
+            )
+            zsend[it, dz, 2, pl.ds(quarter, quarter), :] = two[quarter:]
+            rs_plane(it, dz, 2).start()
+            return carry
+
+        lax.fori_loop(0, lines, group, 0)
 
         def own(dz, carry):
-            mirrored(it, dz, 0)
+            for h in range(2):
+                ag_plane(it, dz, 1 + h).wait_recv()
+                ag_turn(it, dz, h).start()
+            zsend[it, dz, 0] = mirrored(it, dz, 0)
             direct(it, dz, 0)
             return carry
 
@@ -189,7 +238,7 @@
         def reduce(k, carry):
             dz = lines - 1 - k
             block = zsend[it, dz, 0]
-            for d in range(1, planes):
+            for d in range(1, 3):
                 rs_plane(it, dz, d).wait_recv()
                 block = block + zrecv[it, dz, d]
             z2send[it, dz] = block
@@ -202,15 +251,20 @@
 
         lax.fori_loop(0, lines, reduce, 0)
 
-        def rest(dz, carry):
-            def one(d, inner):
-                ag_plane(it, dz, d).wait_recv()
+        def sides(dz, carry):
+            for d in range(1, 3):
                 direct(it, dz, d)
-                return inner
-
-            return lax.fori_loop(1, planes, one, carry)
-
-        lax.fori_loop(0, lines, rest, 0)
+            return carry
+
+        lax.fori_loop(0, lines, sides, 0)
+
+        def last(dz, carry):
+            for h in range(2):
+                ag_turn(it, dz, h).wait_recv()
+            direct(it, dz, 3)
+            return carry
+
+        lax.fori_loop(0, lines, last, 0)
 
         for dc in range(1, cols):
             rpart[it, dc] = fold_tall(total[dc])
@@ -224,24 +278,23 @@
         for dc in range(1, cols):
             col_y(it, dc).wait_recv()
             mine = mine + rrecv[it, dc]
-        return mine, tall
+        return mine + pack_tall(tall)
 
     def step(it, carry):
-        mine, tall = product(it)
+        result = product(it)
 
         @pl.when(it < ITERS - 1)
         def _():
-            gath[lax.rem(it + 1, ITERS), 0, 0] = mine + pack_tall(tall)
+            gath[lax.rem(it + 1, ITERS), 0, 0] = result
 
         @pl.when(it == ITERS - 1)
         def _():
-            half = size // 2
-            out_ref[pl.ds(0, half), :] = mine[:, :vecs] + tall[:half]
-            out_ref[pl.ds(half, half), :] = mine[:, vecs:] + tall[half:]
+            tall = jnp.concatenate([result[:, :vecs], result[:, vecs:]], axis=0)
+            out_ref[:, pl.ds(0, LANES)] = tall[:LANES].T
+            out_ref[:, pl.ds(LANES, size - LANES)] = tall[LANES:].T
 
         return carry
 
-    load.wait()
     lax.fori_loop(0, ITERS, step, 0)
 
     def drain(it, carry):
@@ -253,9 +306,12 @@
             rs_line(it, dz).wait_send()
 
         def plane_sends(dz, inner):
-            for d in range(1, planes):
+            for d in range(1, 3):
                 ag_plane(it, dz, d).wait_send()
                 rs_plane(it, dz, d).wait_send()
+            for h in range(2):
+                ag_turn(it, dz, h).wait_send()
+                rs_turn(it, dz, h).wait_send()
             return inner
 
         return lax.fori_loop(0, lines, plane_sends, carry)
@@ -266,7 +322,7 @@
 def local(rows, cols, vectors, stiff_tiles, tile_coords, tile_valid):
     size, vecs = vectors.shape
     count = stiff_tiles.shape[2]
-    planes = 4 if rows % 4 == 0 else 1
+    planes = 4
     lines = rows // planes
     place = tile_coords[0, 0, :, 0] * rows + tile_coords[0, 0, :, 1]
     hit = (place[None, :] == jnp.arange(rows * cols, dtype=jnp.int32)[:, None]) & (
@@ -279,7 +335,7 @@
     grid = (ITERS, lines, planes)
     return pl.pallas_call(
         functools.partial(kernel, rows, cols, planes),
-        out_shape=jax.ShapeDtypeStruct((size, vecs), f32),
+        out_shape=jax.ShapeDtypeStruct((vecs, size), f32),
         in_specs=[
             pl.BlockSpec(memory_space=pltpu.VMEM),
             pl.BlockSpec(memory_space=pltpu.SMEM),
@@ -300,15 +356,17 @@
             pltpu.VMEM((cols, size, 2 * vecs), f32),
             dma,
             dma(grid), dma(grid),
+            dma((ITERS, lines, 2)), dma((ITERS, lines, 2)),
             dma((ITERS, cols)), dma((ITERS, cols)),
             dma(grid), dma(grid),
+            dma((ITERS, lines, 2)), dma((ITERS, lines, 2)),
             dma((ITERS, lines)), dma((ITERS, lines)),
             dma((ITERS, cols)), dma((ITERS, cols)),
         ],
         compiler_params=pltpu.CompilerParams(
             collective_id=0, has_side_effects=True, vmem_limit_bytes=48 * 1024 * 1024
         ),
-    )(vectors, slots, stiff_tiles[0, 0])
+    )(vectors.T, slots, stiff_tiles[0, 0]).T
 
 
 def solution(mesh):

time: 61.6 us -> 52.2 us (0.85)
  Pallas kernels: 58.2 us -> 49 us
    pallas_call x1, Pallas kernels: 58.2 us -> 49 us  [local(): pl.pallas_call(functools.partial(kernel, rows, cols, planes), out_shape=j...]
    pallas_call x1 -> x0, local copies, waits for them, and re-layouts: 0.71 us -> none  [local(): pl.pallas_call(functools.partial(kernel, rows, cols, planes), out_shape=j...]
    unnamed x1 -> x3, local copies, waits for them, and re-layouts: 0.94 us -> 1.47 us
where the time goes in v2:
time: 52.2 us; the launch traced here: 52 us
  Pallas kernels  49 us (94%)
  other arithmetic  1.53 us (3%)
  local copies, waits for them, and re-layouts  1.47 us (3%)
    pallas_call x1, Pallas kernels, local(): pl.pallas_call(functools.partial(kernel, rows, cols, planes), out_shape=j...  49 us
    unnamed x3, local copies, waits for them, and re-layouts  1.47 us

profile of v2, /device:TPU:0, one launch (start us, length us, event | category | flops | bytes accessed | tf_op | source)
XLA Modules:
  0.0 52.0 jit_solution(1381378466927467695)
XLA Ops:
  0.0 0.8 %add_bitcast_fusion = s32[32]{0:T(128)S(1)} fusion(s32[1,1,32,2]{2,3,1,0:T(2,128)} %param.6), kind=kLoop, calls=%fused_computation.4 | loop fusion | flops 64 | bytes 384 | tf_op jit(solution)/shard_map/add | solution.py:327
  0.8 0.7 %compare_bitcast_fusion = pred[32]{0:T(512)(128)(4,1)S(1)} fusion(s32[1,1,32]{2,1,0:T(1,128)} %param.7), kind=kLoop, calls=%fused_computation.3 | loop fusion | flops 32 | bytes 160 | tf_op jit(solution)/shard_map/gt | solution.py:329
  1.4 0.1 select_reduce_fusion.slot_ref
  1.5 0.0 copy-start
  1.5 0.8 %copy-done = f32[192,64]{0,1:T(8,128)S(1)} copy-done((f32[192,64]{0,1:T(8,128)S(1)}, f32[192,64]{0,1:T(8,128)}, u32[]{:S(2)}) %copy-start) | copy-done | bytes 49176
  2.4 49.0 %shard_map.46 = f32[64,192]{1,0:T(8,128)S(1)} custom-call(f32[64,192]{1,0:T(8,128)S(1)} %bitcast.8, s32[32]{0:T(128)S(1)} %select_reduce_fusion.slot_ref, f32[32,192,192]{2,1,0:T(8,128)} %bitcast.9), custom_call_target="tpu_custom_call" | custom-call | tf_op jit(solution)/shard_map/pallas_call | solution.py:336
  51.4 0.6 %copy.6 = f32[192,64]{0,1:T(8,128)} copy(f32[192,64]{0,1:T(8,128)S(1)} %bitcast.7) | data formatting | bytes 98304
Async XLA Ops:
  1.5 0.8 %copy-start = (f32[192,64]{0,1:T(8,128)S(1)}, f32[192,64]{0,1:T(8,128)}, u32[]{:S(2)}) copy-start(f32[192,64]{0,1:T(8,128)} %param.4) | copy-start | bytes 147460

commit v3 on v2

--- a/solution.py
+++ b/solution.py
@@ -48,13 +48,14 @@
 
 def kernel(
     rows, cols, planes,
-    x_ref, slot_ref, tiles_hbm, out_ref,
+    x_hbm, coords_hbm, valid_hbm, tiles_hbm, out_ref,
+    x_ref, coords, valid, table, slot_ref,
     tiles, gath, rowg, rpart, rrecv, zsend, zrecv, z2send, z2recv, lhs, total,
-    tile_sem, ag_send, ag_recv, at_send, at_recv, cx_send, cx_recv, r1_send, r1_recv, rt_send, rt_recv, r2_send, r2_recv,
+    tile_sem, small_sem, ag_send, ag_recv, at_send, at_recv, cx_send, cx_recv, r1_send, r1_recv, rt_send, rt_recv, r2_send, r2_recv,
     cy_send, cy_recv,
 ):
     lines = rows // planes
-    vecs, size = x_ref.shape
+    vecs, size = x_hbm.shape
     half = size // 2
     quarter = half // 2
     row = lax.axis_index("row")
@@ -65,6 +66,12 @@
     side = plane % 2
 
     load = pltpu.make_async_copy(tiles_hbm, tiles, tile_sem)
+    small = [
+        pltpu.make_async_copy(src, dst, small_sem.at[i])
+        for i, (src, dst) in enumerate(((x_hbm, x_ref), (coords_hbm, coords), (valid_hbm, valid)))
+    ]
+    for copy in small:
+        copy.start()
     load.start()
 
     def flipped(d):
@@ -132,13 +139,24 @@
         pl.semaphore_signal(barrier, inc=1, device_id=plane_peer(d), device_id_type=MESH)
     for dc in range(1, cols):
         pl.semaphore_signal(barrier, inc=1, device_id=col_peer(dc), device_id_type=MESH)
+    for copy in small:
+        copy.wait()
+    place = jnp.where(valid[...] > 0, coords[0:1, :] * rows + coords[1:2, :], -1)
+    spots = (rows * cols, place.shape[1])
+    hit = lax.broadcasted_iota(jnp.int32, spots, 0) == jnp.broadcast_to(place, spots)
+    found = jnp.max(
+        jnp.where(hit, lax.broadcasted_iota(jnp.int32, spots, 1), -1), axis=1, keepdims=True
+    )
+    table[...] = jnp.broadcast_to(found, table.shape)
+    fill = pltpu.make_async_copy(table, slot_ref, small_sem.at[3])
+    fill.start()
     gath[0, 0, 0] = pack_tall(
         jnp.concatenate([x_ref[:, :LANES].T, x_ref[:, LANES:].T], axis=0)
     )
     pl.semaphore_wait(barrier, (lines - 1) + 2 + (cols - 1))
 
     def tile_parts(a, b, keep):
-        slot = slot_ref[a * rows + b]
+        slot = slot_ref[a * rows + b, 0]
         scale = jnp.where(slot >= 0, 1.0, 0.0).astype(jnp.float32) * keep
         block = tiles[jnp.maximum(slot, 0)] * scale
         high = block.astype(jnp.bfloat16)
@@ -183,16 +201,20 @@
         for d in range(1, 3):
             ag_plane(it, 0, d).start()
         lhs[0] = spread(gath[it, 0, 0]).T.astype(jnp.bfloat16)
+        total[...] = jnp.zeros_like(total)
+
+        @pl.when(it == 0)
+        def _():
+            fill.wait()
+            load.wait()
+
+        direct(it, 0, 0)
         for dc in range(1, cols):
             col_x(it, dc).wait_recv()
             lhs[dc] = spread(rowg[it, dc]).T.astype(jnp.bfloat16)
-        total[...] = jnp.zeros_like(total)
-
-        @pl.when(it == 0)
-        def _():
-            load.wait()
-
-        def corner(dz, carry):
+
+        def corner(n, carry):
+            dz = (n + 1) % lines
             zsend[it, dz, 3] = mirrored(it, dz, 3)
             for h in range(2):
                 rs_turn(it, dz, h).start()
@@ -200,13 +222,8 @@
 
         lax.fori_loop(0, lines, corner, 0)
 
-        def group(dz, carry):
-            @pl.when(dz > 0)
-            def _():
-                ag_line(it, dz).wait_recv()
-                for d in range(1, 3):
-                    ag_plane(it, dz, d).start()
-
+        def group(n, carry):
+            dz = (n + 1) % lines
             one = mirrored(it, dz, 1)
             rs_turn(it, dz, 1).wait_recv()
             zsend[it, dz, 1, pl.ds(0, quarter), :] = one[:quarter]
@@ -221,35 +238,39 @@
             )
             zsend[it, dz, 2, pl.ds(quarter, quarter), :] = two[quarter:]
             rs_plane(it, dz, 2).start()
+
+            @pl.when(dz > 0)
+            def _():
+                ag_line(it, dz).wait_recv()
+                for d in range(1, 3):
+                    ag_plane(it, dz, d).start()
+
             return carry
 
         lax.fori_loop(0, lines, group, 0)
 
-        def own(dz, carry):
+        def turn(dz, carry):
             for h in range(2):
                 ag_plane(it, dz, 1 + h).wait_recv()
                 ag_turn(it, dz, h).start()
-            zsend[it, dz, 0] = mirrored(it, dz, 0)
-            direct(it, dz, 0)
-            return carry
-
-        lax.fori_loop(0, lines, own, 0)
-
-        def reduce(k, carry):
-            dz = lines - 1 - k
-            block = zsend[it, dz, 0]
+            return carry
+
+        def own(n, carry):
+            dz = (n + 1) % lines
+            mine = mirrored(it, dz, 0)
             for d in range(1, 3):
                 rs_plane(it, dz, d).wait_recv()
-                block = block + zrecv[it, dz, d]
-            z2send[it, dz] = block
+            z2send[it, dz] = mine + zrecv[it, dz, 1] + zrecv[it, dz, 2]
 
             @pl.when(dz > 0)
             def _():
                 rs_line(it, dz).start()
-
-            return carry
-
-        lax.fori_loop(0, lines, reduce, 0)
+                direct(it, dz, 0)
+
+            turn(n, 0)
+            return carry
+
+        lax.fori_loop(0, lines, own, 0)
 
         def sides(dz, carry):
             for d in range(1, 3):
@@ -324,11 +345,6 @@
     count = stiff_tiles.shape[2]
     planes = 4
     lines = rows // planes
-    place = tile_coords[0, 0, :, 0] * rows + tile_coords[0, 0, :, 1]
-    hit = (place[None, :] == jnp.arange(rows * cols, dtype=jnp.int32)[:, None]) & (
-        tile_valid[0, 0][None, :] > 0
-    )
-    slots = jnp.max(jnp.where(hit, jnp.arange(count, dtype=jnp.int32)[None, :], -1), axis=1)
     block = (size * vecs // LANES, LANES)
     f32 = jnp.float32
     dma = pltpu.SemaphoreType.DMA
@@ -337,12 +353,18 @@
         functools.partial(kernel, rows, cols, planes),
         out_shape=jax.ShapeDtypeStruct((vecs, size), f32),
         in_specs=[
-            pl.BlockSpec(memory_space=pltpu.VMEM),
-            pl.BlockSpec(memory_space=pltpu.SMEM),
+            pl.BlockSpec(memory_space=pl.ANY),
+            pl.BlockSpec(memory_space=pl.ANY),
+            pl.BlockSpec(memory_space=pl.ANY),
             pl.BlockSpec(memory_space=pl.ANY),
         ],
         out_specs=pl.BlockSpec(memory_space=pltpu.VMEM),
         scratch_shapes=[
+            pltpu.VMEM((vecs, size), f32),
+            pltpu.VMEM((2, count), jnp.int32),
+            pltpu.VMEM((1, count), jnp.int32),
+            pltpu.VMEM((rows * cols, LANES), jnp.int32),
+            pltpu.SMEM((rows * cols, LANES), jnp.int32),
             pltpu.VMEM((count, size, size), f32),
             pltpu.VMEM(grid + block, f32),
             pltpu.VMEM((ITERS, cols) + block, f32),
@@ -355,6 +377,7 @@
             pltpu.VMEM((cols, 2 * vecs, size), jnp.bfloat16),
             pltpu.VMEM((cols, size, 2 * vecs), f32),
             dma,
+            dma((4,)),
             dma(grid), dma(grid),
             dma((ITERS, lines, 2)), dma((ITERS, lines, 2)),
             dma((ITERS, cols)), dma((ITERS, cols)),
@@ -366,7 +389,7 @@
         compiler_params=pltpu.CompilerParams(
             collective_id=0, has_side_effects=True, vmem_limit_bytes=48 * 1024 * 1024
         ),
-    )(vectors.T, slots, stiff_tiles[0, 0]).T
+    )(vectors.T, tile_coords[0, 0].T, tile_valid[0], stiff_tiles[0, 0]).T
 
 
 def solution(mesh):

time: 52.2 us -> 48.4 us (0.927)
  Pallas kernels: 49 us -> 45.2 us
  other arithmetic: 1.53 us -> 0 us
  local copies, waits for them, and re-layouts: 1.47 us -> 2.8 us
    pallas_call x1, Pallas kernels: 49 us -> 45.2 us  [local(): pl.pallas_call(functools.partial(kernel, rows, cols, planes), out_shape=j...]
    unnamed x3 -> x7, local copies, waits for them, and re-layouts: 1.47 us -> 2.8 us
    add x1 -> x0, other arithmetic: 0.76 us -> none  [local(): place = tile_coords[0, 0, :, 0] * rows + tile_coords[0, 0, :, 1]]
    gt x1 -> x0, other arithmetic: 0.66 us -> none  [local(): tile_valid[0, 0][None, :] > 0]
where the time goes in v3:
time: 48.4 us; the launch traced here: 48 us
  Pallas kernels  45.2 us (93%)
  local copies, waits for them, and re-layouts  2.8 us (6%)
    pallas_call x1, Pallas kernels, local(): pl.pallas_call(functools.partial(kernel, rows, cols, planes), out_shape=j...  45.2 us
    unnamed x7, local copies, waits for them, and re-layouts  2.8 us

profile of v3, /device:TPU:0, one launch (start us, length us, event | category | flops | bytes accessed | tf_op | source)
XLA Modules:
  0.0 48.0 jit_solution(18003966930593708659)
XLA Ops:
  0.0 0.0 copy-start
  0.0 0.8 %copy-done = f32[192,64]{0,1:T(8,128)S(1)} copy-done((f32[192,64]{0,1:T(8,128)S(1)}, f32[192,64]{0,1:T(8,128)}, u32[]{:S(2)}) %copy-start) | copy-done | bytes 49176
  0.8 0.0 copy-start.1
  0.8 0.7 %copy-done.1 = s32[1,1,32,2]{2,3,1,0:T(2,128)S(1)} copy-done((s32[1,1,32,2]{2,3,1,0:T(2,128)S(1)}, s32[1,1,32,2]{2,3,1,0:T(2,128)}, u32[]{:S(2)}) %copy-start.1) | copy-done | bytes 280
  1.5 0.0 copy-start.2
  1.5 0.7 %copy-done.2 = s32[1,1,32]{2,1,0:T(1,128)S(1)} copy-done((s32[1,1,32]{2,1,0:T(1,128)S(1)}, s32[1,1,32]{2,1,0:T(1,128)}, u32[]{:S(2)}) %copy-start.2) | copy-done | bytes 152
  2.2 45.2 %shard_map.46 = f32[64,192]{1,0:T(8,128)S(1)} custom-call(f32[64,192]{1,0:T(8,128)S(1)} %bitcast.8, s32[2,32]{1,0:T(2,128)S(1)} %bitcast.9, s32[1,32]{1,0:T(1,128)S(1)} %bitcast.10, f32[32,192,192]{2,1,0:T(8,128)} %bitcast.11), custom_call_target="tpu_custom_call" | custom-call | tf_op jit(solution)/shard_map/pallas_call | solution.py:352
  47.4 0.6 %copy.6 = f32[192,64]{0,1:T(8,128)} copy(f32[192,64]{0,1:T(8,128)S(1)} %bitcast.7) | data formatting | bytes 98304
Async XLA Ops:
  0.0 0.8 %copy-start = (f32[192,64]{0,1:T(8,128)S(1)}, f32[192,64]{0,1:T(8,128)}, u32[]{:S(2)}) copy-start(f32[192,64]{0,1:T(8,128)} %param.4) | copy-start | bytes 147460
  0.8 0.7 %copy-start.1 = (s32[1,1,32,2]{2,3,1,0:T(2,128)S(1)}, s32[1,1,32,2]{2,3,1,0:T(2,128)}, u32[]{:S(2)}) copy-start(s32[1,1,32,2]{2,3,1,0:T(2,128)} %param.6) | copy-start | bytes 772
  1.5 0.7 %copy-start.2 = (s32[1,1,32]{2,1,0:T(1,128)S(1)}, s32[1,1,32]{2,1,0:T(1,128)}, u32[]{:S(2)}) copy-start(s32[1,1,32]{2,1,0:T(1,128)} %param.7) | copy-start | bytes 388

commit v4 on v3

--- a/solution.py
+++ b/solution.py
@@ -10,6 +10,7 @@
 ITERS = 2
 MESH = pl.DeviceIdType.MESH
 LANES = 128
+SPLIT, KEEP, READ = range(3)
 
 
 def split(value):
@@ -47,10 +48,10 @@
 
 
 def kernel(
-    rows, cols, planes,
+    rows, cols, planes, kept,
     x_hbm, coords_hbm, valid_hbm, tiles_hbm, out_ref,
     x_ref, coords, valid, table, slot_ref,
-    tiles, gath, rowg, rpart, rrecv, zsend, zrecv, z2send, z2recv, lhs, total,
+    tiles, gath, rowg, rpart, rrecv, zsend, zrecv, z2send, z2recv, lhs, total, parts,
     tile_sem, small_sem, ag_send, ag_recv, at_send, at_recv, cx_send, cx_recv, r1_send, r1_recv, rt_send, rt_recv, r2_send, r2_recv,
     cy_send, cy_recv,
 ):
@@ -155,12 +156,22 @@
     )
     pl.semaphore_wait(barrier, (lines - 1) + 2 + (cols - 1))
 
-    def tile_parts(a, b, keep):
-        slot = slot_ref[a * rows + b, 0]
-        scale = jnp.where(slot >= 0, 1.0, 0.0).astype(jnp.float32) * keep
+    def split_tile(spot):
+        slot = slot_ref[spot, 0]
+        scale = jnp.where(slot >= 0, 1.0, 0.0).astype(jnp.float32)
         block = tiles[jnp.maximum(slot, 0)] * scale
         high = block.astype(jnp.bfloat16)
         low = (block - high.astype(jnp.float32)).astype(jnp.bfloat16)
+        return high, low
+
+    def tile_parts(a, b, mode):
+        spot = a * rows + b
+        if kept and mode == READ:
+            return parts[spot, 0], parts[spot, 1]
+        high, low = split_tile(spot)
+        if kept and mode == KEEP:
+            parts[spot, 0] = high
+            parts[spot, 1] = low
         return high, low
 
     def mirrored(it, dz, d):
@@ -168,9 +179,10 @@
         acc = jnp.zeros((2 * vecs, size), jnp.float32)
         for dc in range(cols):
             a = (col - dc + cols) % cols
-            keep = jnp.where(b == row, 0.0, 1.0).astype(jnp.float32) if dc == 0 else 1.0
-            high, low = tile_parts(a, b, keep)
+            high, low = tile_parts(a, b, KEEP if it == 0 else READ)
             left = lhs[dc]
+            if dc == 0 and d == 0:
+                left = left * jnp.where(b == row, 0.0, 1.0).astype(jnp.bfloat16)
             acc = acc + jnp.dot(left, high, preferred_element_type=jnp.float32)
             acc = acc + jnp.dot(left, low, preferred_element_type=jnp.float32)
         wide = acc[:vecs] + acc[vecs:]
@@ -183,15 +195,21 @@
             axis=0,
         )
 
-    def direct(it, dz, d):
-        b = ((line - dz + lines) % lines) * planes + flipped(d)
-        right = spread(gath[it, dz, d]).astype(jnp.bfloat16)
+    def direct(it, dz, *flips):
+        sums = [None] * cols
+        for d in flips:
+            b = ((line - dz + lines) % lines) * planes + flipped(d)
+            right = spread(gath[it, dz, d]).astype(jnp.bfloat16)
+            for dc in range(cols):
+                high, low = tile_parts(
+                    (col + dc) % cols, b, SPLIT if it == 0 and d == 0 else READ
+                )
+                term = jnp.dot(high, right, preferred_element_type=jnp.float32) + jnp.dot(
+                    low, right, preferred_element_type=jnp.float32
+                )
+                sums[dc] = term if sums[dc] is None else sums[dc] + term
         for dc in range(cols):
-            a = (col + dc) % cols
-            high, low = tile_parts(a, b, 1.0)
-            total[dc] += jnp.dot(high, right, preferred_element_type=jnp.float32) + jnp.dot(
-                low, right, preferred_element_type=jnp.float32
-            )
+            total[dc] += sums[dc]
 
     def product(it):
         for dz in range(1, lines):
@@ -203,8 +221,7 @@
         lhs[0] = spread(gath[it, 0, 0]).T.astype(jnp.bfloat16)
         total[...] = jnp.zeros_like(total)
 
-        @pl.when(it == 0)
-        def _():
+        if it == 0:
             fill.wait()
             load.wait()
 
@@ -258,6 +275,8 @@
         def own(n, carry):
             dz = (n + 1) % lines
             mine = mirrored(it, dz, 0)
+            turn(n, 0)
+            direct(it, n, 1, 2)
             for d in range(1, 3):
                 rs_plane(it, dz, d).wait_recv()
             z2send[it, dz] = mine + zrecv[it, dz, 1] + zrecv[it, dz, 2]
@@ -267,17 +286,9 @@
                 rs_line(it, dz).start()
                 direct(it, dz, 0)
 
-            turn(n, 0)
             return carry
 
         lax.fori_loop(0, lines, own, 0)
-
-        def sides(dz, carry):
-            for d in range(1, 3):
-                direct(it, dz, d)
-            return carry
-
-        lax.fori_loop(0, lines, sides, 0)
 
         def last(dz, carry):
             for h in range(2):
@@ -301,22 +312,14 @@
             mine = mine + rrecv[it, dc]
         return mine + pack_tall(tall)
 
-    def step(it, carry):
+    for it in range(ITERS):
         result = product(it)
-
-        @pl.when(it < ITERS - 1)
-        def _():
-            gath[lax.rem(it + 1, ITERS), 0, 0] = result
-
-        @pl.when(it == ITERS - 1)
-        def _():
+        if it < ITERS - 1:
+            gath[it + 1, 0, 0] = result
+        else:
             tall = jnp.concatenate([result[:, :vecs], result[:, vecs:]], axis=0)
             out_ref[:, pl.ds(0, LANES)] = tall[:LANES].T
             out_ref[:, pl.ds(LANES, size - LANES)] = tall[LANES:].T
-
-        return carry
-
-    lax.fori_loop(0, ITERS, step, 0)
 
     def drain(it, carry):
         for dc in range(1, cols):
@@ -345,12 +348,13 @@
     count = stiff_tiles.shape[2]
     planes = 4
     lines = rows // planes
+    kept = rows * cols * size * size * 4 <= 16 * 1024 * 1024
     block = (size * vecs // LANES, LANES)
     f32 = jnp.float32
     dma = pltpu.SemaphoreType.DMA
     grid = (ITERS, lines, planes)
     return pl.pallas_call(
-        functools.partial(kernel, rows, cols, planes),
+        functools.partial(kernel, rows, cols, planes, kept),
         out_shape=jax.ShapeDtypeStruct((vecs, size), f32),
         in_specs=[
             pl.BlockSpec(memory_space=pl.ANY),
@@ -376,6 +380,7 @@
             pltpu.VMEM((ITERS, lines) + block, f32),
             pltpu.VMEM((cols, 2 * vecs, size), jnp.bfloat16),
             pltpu.VMEM((cols, size, 2 * vecs), f32),
+            pltpu.VMEM((rows * cols if kept else 1, 2, size, size), jnp.bfloat16),
             dma,
             dma((4,)),
             dma(grid), dma(grid),

time: 48.4 us -> 46.3 us (0.957)
  Pallas kernels: 45.2 us -> 43.1 us
    pallas_call x1, Pallas kernels: 45.2 us -> 43.1 us  [local(): pl.pallas_call(functools.partial(kernel, rows, cols, planes, kept), out_s...]
where the time goes in v4:
time: 46.3 us; the launch traced here: 46 us
  Pallas kernels  43.1 us (93%)
  local copies, waits for them, and re-layouts  2.8 us (6%)
    pallas_call x1, Pallas kernels, local(): pl.pallas_call(functools.partial(kernel, rows, cols, planes, kept), out_s...  43.1 us
    unnamed x7, local copies, waits for them, and re-layouts  2.8 us

profile of v4, /device:TPU:0, one launch (start us, length us, event | category | flops | bytes accessed | tf_op | source)
XLA Modules:
  0.0 46.0 jit_solution(2280777812281449596)
XLA Ops:
  0.0 0.0 copy-start
  0.0 0.8 %copy-done = f32[192,64]{0,1:T(8,128)S(1)} copy-done((f32[192,64]{0,1:T(8,128)S(1)}, f32[192,64]{0,1:T(8,128)}, u32[]{:S(2)}) %copy-start) | copy-done | bytes 49176
  0.8 0.0 copy-start.1
  0.8 0.7 %copy-done.1 = s32[1,1,32,2]{2,3,1,0:T(2,128)S(1)} copy-done((s32[1,1,32,2]{2,3,1,0:T(2,128)S(1)}, s32[1,1,32,2]{2,3,1,0:T(2,128)}, u32[]{:S(2)}) %copy-start.1) | copy-done | bytes 280
  1.5 0.0 copy-start.2
  1.5 0.7 %copy-done.2 = s32[1,1,32]{2,1,0:T(1,128)S(1)} copy-done((s32[1,1,32]{2,1,0:T(1,128)S(1)}, s32[1,1,32]{2,1,0:T(1,128)}, u32[]{:S(2)}) %copy-start.2) | copy-done | bytes 152
  2.2 43.1 %shard_map.46 = f32[64,192]{1,0:T(8,128)S(1)} custom-call(f32[64,192]{1,0:T(8,128)S(1)} %bitcast.8, s32[2,32]{1,0:T(2,128)S(1)} %bitcast.9, s32[1,32]{1,0:T(1,128)S(1)} %bitcast.10, f32[32,192,192]{2,1,0:T(8,128)} %bitcast.11), custom_call_target="tpu_custom_call" | custom-call | tf_op jit(solution)/shard_map/pallas_call | solution.py:356
  45.3 0.6 %copy.6 = f32[192,64]{0,1:T(8,128)} copy(f32[192,64]{0,1:T(8,128)S(1)} %bitcast.7) | data formatting | bytes 98304
Async XLA Ops:
  0.0 0.8 %copy-start = (f32[192,64]{0,1:T(8,128)S(1)}, f32[192,64]{0,1:T(8,128)}, u32[]{:S(2)}) copy-start(f32[192,64]{0,1:T(8,128)} %param.4) | copy-start | bytes 147460
  0.8 0.7 %copy-start.1 = (s32[1,1,32,2]{2,3,1,0:T(2,128)S(1)}, s32[1,1,32,2]{2,3,1,0:T(2,128)}, u32[]{:S(2)}) copy-start(s32[1,1,32,2]{2,3,1,0:T(2,128)} %param.6) | copy-start | bytes 772
  1.5 0.7 %copy-start.2 = (s32[1,1,32]{2,1,0:T(1,128)S(1)}, s32[1,1,32]{2,1,0:T(1,128)}, u32[]{:S(2)}) copy-start(s32[1,1,32]{2,1,0:T(1,128)} %param.7) | copy-start | bytes 388
